TPU v7x, 32 devices: a whole 2x2x4 slice. The times are simulated.
32 devices in a mesh: row: 4 (over z), col: 8 (over y, x, core).
Axes of the slice: x: 2, y: 2, z: 4, core: 2. Of those that a mesh axis runs over, the one named last changes fastest.
Arguments:
- tile_values: float32 [512, 512, 512], P(('row', 'col')), may hold values from -6 to 6
- tile_coords: int32 [512, 2], P(('row', 'col')), may hold values from 0 to 3, as said below
- tile_counts: int32 [32], P(('row', 'col')), may hold values from 4 to 16, as said below
- restrict_basis: float32 [8192, 256], P(('row', 'col')), may hold values from -0.25 to 0.25
- prolong_basis: float32 [16384, 256], P(('col', 'row')), may hold values from -0.25 to 0.25
- row_partner: int32 [8, 4], replicated, may hold values from 0 to 3, as said below
- col_partner: int32 [4, 8], replicated, may hold values from 0 to 7, as said below
Outputs:
- coarse: float32 [2048, 4096], P('row', 'col')
Inputs may be any that keep to these rules, and one draw needn't show every extreme that they name: `tile_coords`: within one device's 16 slots no two name the same (block row, block column); first entry below 4, second below 4; dead slots also hold such positions. `tile_counts`: number of leading slots of each device that are live; some device has all 16 live. `row_partner`: each row is a pairing: the partner of a part's partner is the part itself, never the part. `col_partner`: each row is a pairing: the partner of a part's partner is the part itself, never the part.
All inputs are finite; a program needn't handle non-finite values.
Results may differ from a plain program's by a relative error of at most 0.0003.
Values sent between devices are 32-bit elements; how exact they have to be, the bound alone decides.
No kernel may reach another device: no remote copies, remote signals or barrier semaphores. Data moves between devices by JAX's collectives and lax.ppermute only.
A program may use at most 128 MiB of HBM per device.

v0:
```python
import functools

import jax
import jax.numpy as jnp
from jax import lax
from jax.experimental import pallas as pl
from jax.experimental.pallas import tpu as pltpu
from jax.sharding import PartitionSpec as P

F32 = jnp.float32
BF16 = jnp.bfloat16
VMEM_BYTES = 48 * 1024 * 1024
PARAMS = pltpu.CompilerParams(vmem_limit_bytes=VMEM_BYTES)


def split(value):
    high = value.astype(BF16)
    low = (value - high.astype(F32)).astype(BF16)
    return high, low


def dot(left, right):
    return jnp.dot(left, right, preferred_element_type=F32)


def product(left_both, right_high, right_low):
    half = left_both.shape[0] // 2
    total = dot(left_both[half:], right_high)
    total = total + dot(left_both[:half], right_low)
    return total + dot(left_both[:half], right_high)


def div(value, by):
    return lax.div(value, jnp.int32(by))


def rem(value, by):
    return lax.rem(value, jnp.int32(by))


def half_of(given, me, row_partner):
    mate = row_partner[me[1], me[0]]
    return ((mate > me[0]) if given else (me[0] > mate)).astype(jnp.int32)


def tables_kernel(n_row, half_rows, block_cols, me, live, row_partner, slots, mate_slots, sizes):
    columns = Columns(Columns.OWN, n_row, block_cols)
    mate = row_partner[me[1], me[0]]
    places = slots.shape[0]
    per_device = live.shape[0] // n_row
    for table, row in ((slots, me[0]), (mate_slots, mate)):
        for place in range(places):
            table[place] = jnp.int32(-1)
        for slot in range(per_device):
            block_row = live[row * per_device + slot, 0]

            @pl.when(block_row >= 0)
            def _():
                table[block_row * block_cols + live[row * per_device + slot, 1]] = jnp.int32(slot)

    half_cols = columns.half_cols
    for chunk in range(2):
        counts = []
        for table, row, given in ((slots, me[0], True), (mate_slots, mate, False)):
            first_row = half_of(given, me, row_partner) * half_rows
            first_col = (columns.side(row) ^ chunk) * half_cols
            count = jnp.int32(0)
            for index in range(half_rows * half_cols):
                place = (first_row + index % half_rows) * block_cols + first_col + index // half_rows
                count = count + (table[place] >= 0).astype(jnp.int32)
            counts.append(count)
        sizes[chunk] = jnp.maximum(*counts)


def make_tables(me, live, row_partner, n_row, half_rows, block_cols):
    smem = pl.BlockSpec(memory_space=pltpu.SMEM)
    places = 2 * half_rows * block_cols
    return pl.pallas_call(
        functools.partial(tables_kernel, n_row, half_rows, block_cols),
        in_specs=[smem] * 3,
        out_specs=[smem] * 3,
        out_shape=[jax.ShapeDtypeStruct((n,), jnp.int32) for n in (places, places, 2)],
        name="make_tables",
    )(me, live, row_partner)


class ChipBlocks:
    def __init__(self, given, pieces):
        self.given = given
        self.operands = pieces
        self.specs = [pl.BlockSpec(memory_space=pltpu.VMEM)] * len(pieces)

    def near(self, me, row_partner):
        return half_of(self.given, me, row_partner) == div(me[1], 4)

    def row_of(self, group, me, row_partner):
        return div(me[1], 2) ^ (jnp.where(self.near(me, row_partner), 0, 2) + group)

    def load(self, group, me, row_partner, refs, put):
        near = self.near(me, row_partner)
        odd = rem(me[1], 2)
        first, second = refs
        for chip in range(first.shape[0]):
            depth = first.shape[1]
            wanted = (group == chip % 2) & (near == (chip < 2))
            for core in range(2):

                @pl.when(wanted & (odd == core))
                def _():
                    put(first[chip], core * depth)
                    put(second[chip], (1 - core) * depth)


class WholeBlocks:
    def __init__(self, given, rows, tile_order, half_rows):
        self.given = given
        self.half_rows = half_rows
        self.operands = [rows]
        self.specs = [
            pl.BlockSpec(
                (tile_order, rows.shape[1]),
                lambda g, b, me, slots, row_partner: (self.row_of(g, me, row_partner), 0),
            )
        ]

    def row_of(self, group, me, row_partner):
        return half_of(self.given, me, row_partner) * self.half_rows + group

    def load(self, group, me, row_partner, refs, put):
        put(refs[0][...], 0)


def left_kernel(blocks, block_cols, per_step, *refs):
    me, slots, row_partner = refs[:3]
    tile_refs = refs[3 : 3 + per_step]
    q_refs = refs[3 + per_step : -2]
    out, q_both = refs[-2:]
    group, step = pl.program_id(0), pl.program_id(1)
    width = q_both.shape[0] // 2

    @pl.when(step == 0)
    def _():
        def put(value, first):
            high, low = split(value.T)
            q_both[:width, first : first + value.shape[0]] = high
            q_both[width:, first : first + value.shape[0]] = low

        blocks.load(group, me, row_partner, q_refs, put)

    block_row = blocks.row_of(group, me, row_partner)
    for index, tile_ref in enumerate(tile_refs):
        live = slots[block_row * block_cols + step * per_step + index] >= 0
        high, low = split(tile_ref[0])
        total = jnp.where(live, product(q_both[...], high, low), 0.0)
        out[index, 0], out[index, 1] = split(total)


def left_products(me, slots, row_partner, tiles, blocks, half_rows, block_cols):
    _, tile_order, _ = tiles.shape
    width = blocks.operands[0].shape[-1]
    per_step = 2 if block_cols % 2 == 0 else 1

    def tile_spec(index):
        def tile_at(g, b, me, slots, row_partner):
            place = blocks.row_of(g, me, row_partner) * block_cols + b * per_step + index
            return jnp.maximum(slots[place], 0), 0, 0

        return pl.BlockSpec((1, tile_order, tile_order), tile_at)

    def out_at(g, b, me, slots, row_partner):
        return b, 0, rem(blocks.row_of(g, me, row_partner), half_rows), 0

    return pl.pallas_call(
        functools.partial(left_kernel, blocks, block_cols, per_step),
        grid_spec=pltpu.PrefetchScalarGridSpec(
            num_scalar_prefetch=3,
            grid=(half_rows, block_cols // per_step),
            in_specs=[tile_spec(index) for index in range(per_step)] + blocks.specs,
            out_specs=pl.BlockSpec((per_step, 2, width, tile_order), out_at),
            scratch_shapes=[pltpu.VMEM((2 * width, tile_order), BF16)],
        ),
        out_shape=jax.ShapeDtypeStruct((block_cols, 2, half_rows * width, tile_order), BF16),
        compiler_params=PARAMS,
        cost_estimate=pl.CostEstimate(
            flops=12 * half_rows * block_cols * width * tile_order * tile_order,
            bytes_accessed=4 * half_rows * block_cols * tile_order * (tile_order + width),
            transcendentals=0,
        ),
        name="left_products",
    )(me, slots, row_partner, *[tiles] * per_step, *blocks.operands)


class Columns:
    OWN, FAR, KEPT = range(3)

    def __init__(self, kind, n_row, block_cols):
        self.kind = kind
        self.n_row = n_row
        self.half_cols = block_cols // 2
        self.steps = block_cols if kind == self.KEPT else self.half_cols

    def side(self, row):
        return div(2 * row, self.n_row)

    def half(self, step, me, col_partner):
        if self.kind == self.KEPT:
            goes_on = (me[1] < col_partner[me[0], me[1]]).astype(jnp.int32)
            return goes_on ^ div(step, self.half_cols)
        return self.side(me[0]) ^ (1 if self.kind == self.FAR else 0)

    def column(self, step, me, col_partner):
        return self.half(step, me, col_partner) * self.half_cols + rem(step, self.half_cols)


def packed_place(slots, first_row, first_col, half_rows, half_cols, block_cols, block):
    before = here = count = jnp.int32(0)
    for index in range(half_rows * half_cols):
        place = (first_row + index % half_rows) * block_cols + first_col + index // half_rows
        flag = (slots[place] >= 0).astype(jnp.int32)
        before = before + jnp.where(index < block, flag, 0)
        here = here + jnp.where(index == block, flag, 0)
        count = count + flag
    return jnp.where(here == 1, before, count + block - before), here == 1


def right_kernel(columns, block_cols, half_rows, shard_places, groups, *refs):
    me, slots, row_partner, col_partner, w_ref = refs[:5]
    pieces = refs[5 : 5 + sum(groups)]
    step = pl.program_id(0)
    tile_order = w_ref.shape[3]
    depth, width = pieces[0].shape
    packs = columns.kind != Columns.KEPT
    outs = refs[5 + sum(groups) : -3 if packs else -2]
    p_high, p_low = refs[-2:]

    @pl.when(step == 0)
    def _():
        at = 0
        for place, count in zip(shard_places(me), groups):
            value = pieces[at][...]
            for other in range(1, count):
                value = value + pieces[at + other][...]
            at += count
            rows = pl.ds(pl.multiple_of(place * depth, depth), depth)
            p_high[rows, :], p_low[rows, :] = split(value)

    column = columns.column(step, me, col_partner)
    rows = pl.ds(pl.multiple_of(column * tile_order, tile_order), tile_order)
    both = w_ref[0].reshape(2 * w_ref.shape[2], tile_order)
    block = product(both, p_high[rows, :], p_low[rows, :])
    half_cols = columns.half_cols
    if not packs:
        first, second = outs

        @pl.when(step < half_cols)
        def _():
            first[...] = block

        @pl.when(step >= half_cols)
        def _():
            second[...] = block

        return
    packed = refs[-3]
    first_row = half_of(True, me, row_partner) * half_rows
    first_col = columns.half(step, me, col_partner) * half_cols
    for row in range(half_rows):
        place, _ = packed_place(
            slots, first_row, first_col, half_rows, half_cols, block_cols, step * half_rows + row
        )
        packed[place] = block[row * width : (row + 1) * width]

    @pl.when(step == half_cols - 1)
    def _():
        count = outs[0].shape[0]
        outs[0][...] = packed[:count]
        for index, out in enumerate(outs[1:]):
            out[...] = packed[count + index]


def right_products(kind, me, slots, row_partner, col_partner, w, shards, shard_places, n_row, half_rows):
    block_cols, _, height, tile_order = w.shape
    columns = Columns(kind, n_row, block_cols)
    half_cols = columns.half_cols
    depth, width = shards[0][0].shape
    groups = [len(shard) for shard in shards]
    blocks = half_rows * half_cols
    p_rows = block_cols * tile_order

    def w_at(i, me, slots, row_partner, col_partner):
        return columns.column(i, me, col_partner), 0, 0, 0

    def quarter(first):
        return pl.BlockSpec(
            (height, width), lambda i, *_: (0, jnp.clip(i - first, 0, half_cols - 1))
        )

    scratch = [pltpu.VMEM((p_rows, width), BF16)] * 2
    if kind == Columns.KEPT:
        shapes = [(height, half_cols * width)] * 2
        out_specs = [quarter(0), quarter(half_cols)]
    else:
        most = max(1, blocks * 3 // 4)
        shapes = [(most, width, width)] + [(width, width)] * (blocks - most)
        out_specs = [pl.BlockSpec(shape, lambda i, *_, n=len(shape): (0,) * n) for shape in shapes]
        scratch = [pltpu.VMEM((blocks, width, width), F32)] + scratch
    return pl.pallas_call(
        functools.partial(right_kernel, columns, block_cols, half_rows, shard_places, groups),
        grid_spec=pltpu.PrefetchScalarGridSpec(
            num_scalar_prefetch=4,
            grid=(columns.steps,),
            in_specs=[pl.BlockSpec((1, 2, height, tile_order), w_at)]
            + [pl.BlockSpec(memory_space=pltpu.VMEM)] * sum(groups),
            out_specs=out_specs,
            scratch_shapes=scratch,
        ),
        out_shape=[jax.ShapeDtypeStruct(shape, F32) for shape in shapes],
        compiler_params=PARAMS,
        cost_estimate=pl.CostEstimate(
            flops=6 * columns.steps * height * width * tile_order,
            bytes_accessed=4 * columns.steps * height * (tile_order + width),
            transcendentals=0,
        ),
        name="right_products",
    )(me, slots, row_partner, col_partner, w, *[piece for shard in shards for piece in shard])


def sum_kernel(columns, second, half_rows, block_cols, arrays, *refs):
    me, mate_slots, row_partner, col_partner, kept_ref = refs[:5]
    chunks = refs[5 : 5 + arrays]
    sections, out = refs[5 + arrays : -1], refs[-1]
    half_cols = columns.half_cols
    first_row = half_of(False, me, row_partner) * half_rows
    half = columns.half(half_cols if second else 0, me, col_partner)
    chunk = columns.side(row_partner[me[1], me[0]]) ^ half
    place, live = packed_place(
        mate_slots, first_row, half * half_cols, half_rows, half_cols, block_cols, pl.program_id(0)
    )
    total = kept_ref[...]
    for section in sections:
        total = total + section[...]

    @pl.when(jnp.logical_not(live))
    def _():
        out[...] = total

    for which in range(2):
        first, *singles = chunks[which * arrays // 2 : (which + 1) * arrays // 2]
        count = first.shape[0]

        @pl.when(live & (chunk == which) & (place < count))
        def _():
            out[...] = total + first[place]

        for index, single in enumerate(singles):

            @pl.when(live & (chunk == which) & (place == count + index))
            def _():
                out[...] = total + single[...]


def sum_blocks(second, tables, n_row, half_rows, block_cols, kept, chunks, section=None):
    columns = Columns(Columns.KEPT, n_row, block_cols)
    half_cols = columns.half_cols
    height, both = kept.shape
    width = both // half_cols
    block = pl.BlockSpec((width, width), lambda i, *_: (rem(i, half_rows), div(i, half_rows)))
    sections = [] if section is None else [section]
    return pl.pallas_call(
        functools.partial(sum_kernel, columns, second, half_rows, block_cols, len(chunks)),
        grid_spec=pltpu.PrefetchScalarGridSpec(
            num_scalar_prefetch=4,
            grid=(half_rows * half_cols,),
            in_specs=[block]
            + [pl.BlockSpec(memory_space=pltpu.VMEM)] * len(chunks)
            + [block] * len(sections),
            out_specs=block,
        ),
        out_shape=jax.ShapeDtypeStruct((height, both), F32),
        compiler_params=PARAMS,
        name="sum_blocks",
    )(*tables, kept, *chunks, *sections)


def flip(value, axis, size, mask):
    return lax.ppermute(value, axis, [(i, i ^ mask) for i in range(size)])


def near_prolong(shard, axis, size):
    if size != 4:
        return []
    return [flip(shard, axis, size, 1), lax.ppermute(shard, axis, [(1, 2), (2, 1)])]


def gather_prolong(shard, near, axis, size):
    if size != 4:
        gathered = lax.all_gather(shard, axis)
        every = [[gathered[i]] for i in range(size)], lambda me: list(range(size))
        return every, every
    mate, over = near
    mate_over = lax.ppermute(mate, axis, [(1, 2), (2, 1)])
    handed = lax.ppermute(over, axis, [(1, 0), (2, 3)])
    mate_handed = lax.ppermute(mate, axis, [(2, 0), (1, 3)])

    def far_places(me):
        return [jnp.where(me[0] < 2, 2, 1), jnp.where(me[0] < 2, 3, 0)]

    own = [[shard], [mate]], lambda me: [me[0], me[0] ^ 1]
    return own, ([[over, handed], [mate_over, mate_handed]], far_places)


def chip_restrict(shard, axis, size):
    over_x = flip(shard, axis, size, 2)
    over_y = flip(shard, axis, size, 4)
    return [shard, over_x, over_y, flip(over_x, axis, size, 4)]


def pair_switch(mine, mate, size, branch, operand, sizes=(None,), choice=0):
    branches = [functools.partial(branch, mask, each) for mask in range(1, size) for each in sizes]
    if len(branches) == 1:
        return branches[0](operand)
    return lax.switch(((mine ^ mate) - 1) * len(sizes) + choice, branches, operand)


def solution(mesh):
    n_row = mesh.shape["row"]
    n_col = mesh.shape["col"]

    def body(tiles, coords, counts, restrict, prolong, row_partner, col_partner):
        tile_order = tiles.shape[1]
        block_rows = restrict.shape[0] * n_col // tile_order
        block_cols = prolong.shape[0] * n_row // tile_order
        half_rows, half_cols = block_rows // 2, block_cols // 2
        row = lax.axis_index("row").astype(jnp.int32)
        col = lax.axis_index("col").astype(jnp.int32)
        me = jnp.stack([row, col])

        row_mate = row_partner[col, row]
        col_mate = col_partner[row, col]

        slot_ids = jnp.arange(tiles.shape[0], dtype=jnp.int32)
        live = lax.all_gather(
            jnp.where(slot_ids[:, None] < counts[0], coords, -1), "row", axis=0, tiled=True
        )
        near = near_prolong(prolong, "row", n_row)
        slots, mate_slots, sizes = make_tables(me, live, row_partner, n_row, half_rows, block_cols)
        by_chip = n_col == 8 and block_rows == 4 and tile_order == 2 * restrict.shape[0]
        if by_chip:
            pieces = chip_restrict(restrict, "col", n_col)
            pieces, near, slots = lax.optimization_barrier((pieces, near, slots))
            mine = jnp.stack(pieces)
            q_pieces = [mine, flip(mine, "col", n_col, 1)]
        else:
            q_rows = lax.all_gather(restrict, "col", axis=0, tiled=True)
        own_shards, far_shards = gather_prolong(prolong, near, "row", n_row)

        def left(given):
            if by_chip:
                blocks = ChipBlocks(given, q_pieces)
            else:
                blocks = WholeBlocks(given, q_rows, tile_order, half_rows)
            return left_products(me, slots, row_partner, tiles, blocks, half_rows, block_cols)

        def right(kind, w, shards, places):
            return right_products(
                kind, me, slots, row_partner, col_partner, w, shards, places, n_row, half_rows
            )

        def swap_chunk(beside, mask, extra, chunk):
            received = [
                flip(array, "row", n_row, mask) if index <= extra else array
                for index, array in enumerate(chunk)
            ]
            return received, beside()

        def swap_section(mask, _, section):
            return flip(section, "col", n_col, mask)

        def exchange(size, chunk, beside):
            choice = jnp.clip(size - chunk[0].shape[0], 0, len(chunk) - 1)
            branch = functools.partial(swap_chunk, beside)
            return pair_switch(row, row_mate, n_row, branch, chunk, tuple(range(len(chunk))), choice)

        w = left(True)
        own = right(Columns.OWN, w, *own_shards)
        own, w_kept = exchange(sizes[0], own, lambda: left(False))
        far_pieces, own = lax.optimization_barrier((far_shards[0], own))
        far = right(Columns.FAR, w, far_pieces, far_shards[1])
        if n_row == 4:
            every = own_shards[0] + far_pieces, lambda me: own_shards[1](me) + far_shards[1](me)
        else:
            every = own_shards
        far, kept = exchange(sizes[1], far, lambda: right(Columns.KEPT, w_kept, *every))
        chunks = list(own) + list(far)
        add = functools.partial(sum_blocks, n_row=n_row, half_rows=half_rows, block_cols=block_cols)
        tables = (me, mate_slots, row_partner, col_partner)
        section = add(False, tables, kept=kept[0], chunks=chunks)
        section = pair_switch(col, col_mate, n_col, swap_section, section)
        return add(True, tables, kept=kept[1], chunks=chunks, section=section)

    in_specs = (
        P(("row", "col"), None, None),
        P(("row", "col"), None),
        P(("row", "col")),
        P(("row", "col"), None),
        P(("col", "row"), None),
        P(),
        P(),
    )
    return jax.shard_map(
        body, mesh=mesh, in_specs=in_specs, out_specs=P("row", "col"), check_vma=False
    )
```

profile of v0, /device:TPU:22, one launch (start us, length us, event | category | flops | bytes accessed | tf_op | source)
XLA Modules:
  0.0 183.6 jit_solution(6179723065936630574)
XLA Ops:
  0.5 1.6 collective-permute-start.28
  2.1 1.9 %collective-permute-start.29 = (f32[512,256]{1,0:T(8,128)}, f32[512,256]{1,0:T(8,128)}, u32[]{:S(2)}, u32[]{:S(2)}) collective-permute-start(f32[512,256]{1,0:T(8,128)} %refs_5_.1), channel_id=1, source_target_pairs={{8,16},{16,8},{9,17},{17,9},{10,18},{18,10},{11,19},{19,11},{12,20... | collective-permute-start | bytes 1572872 | tf_op jit(solution)/shard_map/ppermute | solution.py:392
  4.6 1.4 copy.30.row_partner.refs_2_
  6.6 1.6 collective-permute-done.25
  9.4 9.8 %all-gather = s32[4,16,2]{1,2,0:T(2,128)S(1)} all-gather(s32[1,16,2]{1,2,0:T(2,128)S(1)} %select_bitcast_fusion), channel_id=1, replica_groups=mesh['row'=4,'col'=8] {'row'}, dimensions={0}, use_global_device_ids=true | all-gather | bytes 640 | tf_op jit(solution)/shard_map/all_gather | solution.py:442
  19.3 0.7 copy.48
  20.1 2.0 %make_tables.1 = (s32[16]{0:T(128)S(1)}, s32[16]{0:T(128)}, s32[2]{0:T(128)}) custom-call(s32[2]{0:T(128)S(1)} %pad_add_fusion.me.refs_0_, s32[64,2]{1,0:T(8,128)} %bitcast.19, s32[8,4]{1,0:T(8,128)} %copy.30.row_partner.refs_2_), custom_call_target="tpu_custom_call" | custom-call | tf_op jit(solution)/shard_map/make_tables/pallas_call | solution.py:78
  22.1 1.0 pad_maximum_fusion.refs_5_
  23.2 1.3 dynamic_slice.6
  25.1 1.4 fusion
  27.8 1.3 dynamic_slice.7
  29.7 1.9 %collective-permute-start.32 = (f32[512,256]{1,0:T(8,128)S(1)}, f32[512,256]{1,0:T(8,128)}, u32[]{:S(2)}, u32[]{:S(2)}) collective-permute-start(f32[512,256]{1,0:T(8,128)S(1)} %collective-permute-done.28.refs_6_), channel_id=1, source_target_pairs={{8,16},{16,8},{9,17},{17,9},{10,18},{18,10},{11,19},{19,11},{12,20... | collective-permute-start | bytes 1572872 | tf_op jit(solution)/shard_map/ppermute | solution.py:401
  31.6 3.9 %collective-permute-start.33 = (f32[512,256]{1,0:T(8,128)S(1)}, f32[512,256]{1,0:T(8,128)}, u32[]{:S(2)}, u32[]{:S(2)}) collective-permute-start(f32[512,256]{1,0:T(8,128)S(1)} %collective-permute-done.28.refs_6_), channel_id=1, source_target_pairs={{16,0},{8,24},{17,1},{9,25},{18,2},{10,26},{19,3},{11,27},{20,4},{... | collective-permute-start | bytes 1572872 | tf_op jit(solution)/shard_map/ppermute | solution.py:403
  35.5 2.1 %collective-permute-start.31 = (f32[512,256]{1,0:T(8,128)}, f32[512,256]{1,0:T(8,128)}, u32[]{:S(2)}, u32[]{:S(2)}) collective-permute-start(f32[512,256]{1,0:T(8,128)} %collective-permute-done.29.refs_5_), channel_id=1, source_target_pairs={{8,0},{16,24},{9,1},{17,25},{10,2},{18,26},{11,3},{19,27},{12,4},{... | collective-permute-start | bytes 1572872 | tf_op jit(solution)/shard_map/ppermute | solution.py:402
  38.3 7.5 %left_products.13.refs_4_ = bf16[4,2,512,512]{3,2,1,0:T(8,128)(2,1)S(1)} custom-call(s32[2]{0:T(128)S(1)} %pad_add_fusion.me.refs_0_, s32[16]{0:T(128)S(1)} %get-tuple-element.440.refs_1_, s32[8,4]{1,0:T(8,128)S(1)} %copy-done.2, f32[16,512,512]{2,1,0:T(8,128)} %refs_4_.1, f32[16,512,512]{2,1,0:T(8,128)} %refs_4_.1, ...), custom_call_target="tpu_custom_call" | custom-call | flops 6442450944 | bytes 12582912 | tf_op jit(solution)/shard_map/left_products/pallas_call | solution.py:173
  45.8 3.1 %right_products.14 = (f32[3,256,256]{2,1,0:T(8,128)}, f32[256,256]{1,0:T(8,128)}) custom-call(s32[2]{0:T(128)S(1)} %pad_add_fusion.me.refs_0_, s32[16]{0:T(128)S(1)} %get-tuple-element.440.refs_1_, s32[8,4]{1,0:T(8,128)S(1)} %copy-done.2, s32[4,8]{1,0:T(4,128)S(1)} %copy-done.9, bf16[4,2,512,512]{3,2,1,0:T(8,128)(2,1)S(1)} %left_products.13.refs_4_, ...), custom_call_target="tpu_custom_call" | custom-call | flops 805306368 | bytes 3145728 | tf_op jit(solution)/shard_map/right_products/pallas_call | solution.py:307
  48.9 2.0 %copy-done = bf16[4,2,512,512]{3,2,1,0:T(8,128)(2,1)} copy-done((bf16[4,2,512,512]{3,2,1,0:T(8,128)(2,1)}, bf16[4,2,512,512]{3,2,1,0:T(8,128)(2,1)S(1)}, u32[]{:S(2)}) %copy-start) | copy-done | bytes 4194328
  50.9 61.2 %conditional.3 = (f32[3,256,256]{2,1,0:T(8,128)}, f32[256,256]{1,0:T(8,128)}, bf16[4,2,512,512]{3,2,1,0:T(8,128)(2,1)S(1)}) conditional(s32[]{:T(128)} %clamp.10, (f32[3,256,256]{2,1,0:T(8,128)}, s32[2]{0:T(128)S(1)}, s32[16]{0:T(128)S(1)}, s32[8,4]{0,1:T(4,128)S(1)}, f32[16,512,512]{2,1,0:T(8,128)}, ...), branch_computations={%region_0.1_spmd, %region_1.2_spmd, %region_2.3_spmd, %region_3.4_... | conditional | flops 6442450944 | bytes 17301864 | solution.py:422
  50.9 2.9 %collective-permute-start.5 = (f32[256,256]{1,0:T(8,128)}, f32[256,256]{1,0:T(8,128)S(1)}, u32[]{:S(2)}, u32[]{:S(2)}) collective-permute-start(f32[256,256]{1,0:T(8,128)} %get-tuple-element.297), channel_id=1, source_target_pairs={{0,16},{8,24},{16,0},{24,8},{1,17},{9,25},{17,1},{25,9},{2,18},{10... | collective-permute-start | bytes 786440 | tf_op jit(solution)/shard_map/cond/branch_3_fun/ppermute | solution.py:386
  53.9 7.8 %left_products.10 = bf16[4,2,512,512]{3,2,1,0:T(8,128)(2,1)S(1)} custom-call(s32[2]{0:T(128)S(1)} %get-tuple-element.298.refs_0_, s32[16]{0:T(128)S(1)} %get-tuple-element.299.refs_1_, s32[8,4]{1,0:T(8,128)S(1)} %copy.36.refs_2_, f32[16,512,512]{2,1,0:T(8,128)} %get-tuple-element.301.refs_3_.refs_4_, f32[16,512,512]{2,1,0:T(8,128)} %get-tuple-element.301.refs_3_.refs_4_, ...), custom_call_target="tpu_custom_call" | custom-call | flops 6442450944 | bytes 12582912 | tf_op jit(solution)/shard_map/cond/branch_3_fun/left_products/pallas_call | solution.py:173
  61.6 49.7 %collective-permute-done.5 = f32[256,256]{1,0:T(8,128)S(1)} collective-permute-done((f32[256,256]{1,0:T(8,128)}, f32[256,256]{1,0:T(8,128)S(1)}, u32[]{:S(2)}, u32[]{:S(2)}) %collective-permute-start.5) | collective-permute-done | bytes 262176 | tf_op jit(solution)/shard_map/cond/branch_3_fun/ppermute | solution.py:386
  112.0 2.0 %copy-done.5 = bf16[4,2,512,512]{3,2,1,0:T(8,128)(2,1)} copy-done((bf16[4,2,512,512]{3,2,1,0:T(8,128)(2,1)}, bf16[4,2,512,512]{3,2,1,0:T(8,128)(2,1)S(1)}, u32[]{:S(2)}) %copy-start.5) | copy-done | bytes 4194328
  114.0 2.2 %copy-done.1 = bf16[4,2,512,512]{3,2,1,0:T(8,128)(2,1)S(1)} copy-done((bf16[4,2,512,512]{3,2,1,0:T(8,128)(2,1)S(1)}, bf16[4,2,512,512]{3,2,1,0:T(8,128)(2,1)}, u32[]{:S(2)}) %copy-start.1) | copy-done | bytes 4194328
  116.2 4.5 %right_products.15 = (f32[3,256,256]{2,1,0:T(8,128)}, f32[256,256]{1,0:T(8,128)S(1)}) custom-call(s32[2]{0:T(128)S(1)} %pad_add_fusion.me.refs_0_, s32[16]{0:T(128)S(1)} %get-tuple-element.440.refs_1_, s32[8,4]{1,0:T(8,128)S(1)} %copy-done.3, s32[4,8]{1,0:T(4,128)S(1)} %copy-done.9, bf16[4,2,512,512]{3,2,1,0:T(8,128)(2,1)S(1)} %copy-done.1, ...), custom_call_target="tpu_custom_call" | custom-call | flops 805306368 | bytes 3145728 | tf_op jit(solution)/shard_map/right_products/pallas_call | solution.py:307
  120.7 30.5 %conditional.4 = (f32[3,256,256]{2,1,0:T(8,128)}, f32[256,256]{1,0:T(8,128)S(1)}, f32[512,512]{1,0:T(8,128)S(1)}, f32[512,512]{1,0:T(8,128)}) conditional(s32[]{:T(128)} %clamp.9, (f32[3,256,256]{2,1,0:T(8,128)}, s32[2]{0:T(128)S(1)}, s32[16]{0:T(128)S(1)}, s32[8,4]{0,1:T(4,128)S(1)}, s32[4,8]{1,0:T(4,128)S(1)}, ...), branch_computations={%region_6.7_spmd, %region_7.8_spmd, %region_8.9_spmd, %region_9.10... | conditional | flops 1610612736 | bytes 11010416 | solution.py:422
  120.7 3.3 %collective-permute-start.12 = (f32[3,256,256]{2,1,0:T(8,128)}, f32[3,256,256]{2,1,0:T(8,128)}, u32[]{:S(2)}, u32[]{:S(2)}) collective-permute-start(f32[3,256,256]{2,1,0:T(8,128)} %get-tuple-element.350), channel_id=1, source_target_pairs={{0,16},{8,24},{16,0},{24,8},{1,17},{9,25},{17,1},{25,9},{2,18},{10... | collective-permute-start | bytes 2359304 | tf_op jit(solution)/shard_map/cond/branch_2_fun/ppermute | solution.py:386
  124.1 7.0 %right_products.10 = (f32[512,512]{1,0:T(8,128)S(1)}, f32[512,512]{1,0:T(8,128)}) custom-call(s32[2]{0:T(128)S(1)} %get-tuple-element.352.refs_0_, s32[16]{0:T(128)S(1)} %get-tuple-element.353.refs_1_, s32[8,4]{1,0:T(8,128)S(1)} %copy.42.refs_2_, s32[4,8]{1,0:T(4,128)S(1)} %get-tuple-element.355.refs_3_, ...), custom_call_target="tpu_custom_call" | custom-call | flops 1610612736 | bytes 6291456 | tf_op jit(solution)/shard_map/cond/branch_2_fun/right_products/pallas_call | solution.py:307
  131.1 20.1 %collective-permute-done.12 = f32[3,256,256]{2,1,0:T(8,128)} collective-permute-done((f32[3,256,256]{2,1,0:T(8,128)}, f32[3,256,256]{2,1,0:T(8,128)}, u32[]{:S(2)}, u32[]{:S(2)}) %collective-permute-start.12) | collective-permute-done | bytes 786464 | tf_op jit(solution)/shard_map/cond/branch_2_fun/ppermute | solution.py:386
  151.3 2.7 %sum_blocks.2 = f32[512,512]{1,0:T(8,128)S(1)} custom-call(s32[2]{0:T(128)S(1)} %pad_add_fusion.me.refs_0_, s32[16]{0:T(128)S(1)} %copy-done.4, s32[8,4]{1,0:T(8,128)S(1)} %copy-done.3, s32[4,8]{1,0:T(4,128)S(1)} %copy-done.9, f32[512,512]{1,0:T(8,128)S(1)} %get-tuple-element.463.refs_4_, f32[3,256,256]{2,1,0:T(8,128)} %get-tuple-element.459.refs_5_, ...), custom_call_target="tpu_custom_call" | custom-call | tf_op jit(solution)/shard_map/sum_blocks/pallas_call | solution.py:369
  154.0 24.9 %conditional.5 = (f32[512,512]{1,0:T(8,128)}) conditional(s32[]{:T(128)} %clamp.11, f32[512,512]{1,0:T(8,128)S(1)} %sum_blocks.2, f32[512,512]{1,0:T(8,128)S(1)} %sum_blocks.2, f32[512,512]{1,0:T(8,128)S(1)} %sum_blocks.2, f32[512,512]{1,0:T(8,128)S(1)} %sum_blocks.2, f32[512,512]{1,0:T(8,128)S(1)} %sum_blocks.2, ...), branch_computations={%region_12.13_spmd, %region_13.14_spmd, %region_14.15_spmd, %regio... | conditional | bytes 4194352 | solution.py:422
  154.1 24.7 %collective-permute-done.21 = f32[512,512]{1,0:T(8,128)} collective-permute-done((f32[512,512]{1,0:T(8,128)S(1)}, f32[512,512]{1,0:T(8,128)}, u32[]{:S(2)}, u32[]{:S(2)}) %collective-permute-start.21) | collective-permute-done | bytes 1048608 | tf_op jit(solution)/shard_map/cond/branch_3_fun/ppermute | solution.py:386
  178.8 4.8 %sum_blocks.3 = f32[512,512]{1,0:T(8,128)} custom-call(s32[2]{0:T(128)S(1)} %pad_add_fusion.me.refs_0_, s32[16]{0:T(128)S(1)} %copy-done.4, s32[8,4]{1,0:T(8,128)S(1)} %copy-done.3, s32[4,8]{1,0:T(4,128)S(1)} %copy-done.9, f32[512,512]{1,0:T(8,128)S(1)} %copy-done.7, f32[3,256,256]{2,1,0:T(8,128)} %get-tuple-element.459.refs_5_, ...), custom_call_target="tpu_custom_call" | custom-call | tf_op jit(solution)/shard_map/sum_blocks/pallas_call | solution.py:369
  (38 shorter events, 4.1 us)
Async XLA Ops:
  0.0 8.3 %collective-permute-start.25 = (f32[256,256]{1,0:T(8,128)}, f32[256,256]{1,0:T(8,128)S(1)}, u32[]{:S(2)}, u32[]{:S(2)}) collective-permute-start(f32[256,256]{1,0:T(8,128)} %param.29), channel_id=1, source_target_pairs={{0,2},{1,3},{2,0},{3,1},{4,6},{5,7},{6,4},{7,5},{8,10},{9,11},{10,... | collective-permute-start | bytes 786440 | tf_op jit(solution)/shard_map/ppermute | solution.py:386
  0.5 21.5 %collective-permute-start.28 = (f32[512,256]{1,0:T(8,128)}, f32[512,256]{1,0:T(8,128)S(1)}, u32[]{:S(2)}, u32[]{:S(2)}) collective-permute-start(f32[512,256]{1,0:T(8,128)} %refs_5_.1), channel_id=1, source_target_pairs={{0,8},{8,0},{16,24},{24,16},{1,9},{9,1},{17,25},{25,17},{2,10},{10... | collective-permute-start | bytes 1572872 | tf_op jit(solution)/shard_map/ppermute | solution.py:386
  2.1 20.0 %collective-permute-start.29 = (f32[512,256]{1,0:T(8,128)}, f32[512,256]{1,0:T(8,128)}, u32[]{:S(2)}, u32[]{:S(2)}) collective-permute-start(f32[512,256]{1,0:T(8,128)} %refs_5_.1), channel_id=1, source_target_pairs={{8,16},{16,8},{9,17},{17,9},{10,18},{18,10},{11,19},{19,11},{12,20... | collective-permute-start | bytes 1572872 | tf_op jit(solution)/shard_map/ppermute | solution.py:392
  4.0 18.0 %collective-permute-start.26 = (f32[256,256]{1,0:T(8,128)}, f32[256,256]{1,0:T(8,128)S(1)}, u32[]{:S(2)}, u32[]{:S(2)}) collective-permute-start(f32[256,256]{1,0:T(8,128)} %param.29), channel_id=1, source_target_pairs={{0,4},{1,5},{2,6},{3,7},{4,0},{5,1},{6,2},{7,3},{8,12},{9,13},{10,... | collective-permute-start | bytes 786440 | tf_op jit(solution)/shard_map/ppermute | solution.py:386
  8.3 13.8 %collective-permute-start.27 = (f32[256,256]{1,0:T(8,128)S(1)}, f32[256,256]{1,0:T(8,128)S(1)}, u32[]{:S(2)}, u32[]{:S(2)}) collective-permute-start(f32[256,256]{1,0:T(8,128)S(1)} %collective-permute-done.25), channel_id=1, source_target_pairs={{0,4},{1,5},{2,6},{3,7},{4,0},{5,1},{6,2},{7,3},{8,12},{9,13},{10,... | collective-permute-start | bytes 786440 | tf_op jit(solution)/shard_map/ppermute | solution.py:386
  23.1 14.5 %collective-permute-start.30 = (f32[4,256,256]{2,1,0:T(8,128)S(1)}, f32[4,256,256]{2,1,0:T(8,128)S(1)}, u32[]{:S(2)}, u32[]{:S(2)}) collective-permute-start(f32[4,256,256]{2,1,0:T(8,128)S(1)} %pad_maximum_fusion.refs_5_), channel_id=1, source_target_pairs={{0,1},{1,0},{2,3},{3,2},{4,5},{5,4},{6,7},{7,6},{8,9},{9,8},{10,11... | collective-permute-start | bytes 3145736 | tf_op jit(solution)/shard_map/ppermute | solution.py:386
  29.7 16.1 %copy-start.9 = (s32[4,8]{1,0:T(4,128)S(1)}, s32[4,8]{1,0:T(4,128)}, u32[]{:S(2)}) copy-start(s32[4,8]{1,0:T(4,128)} %refs_3_.9) | copy-start | bytes 388
  29.7 82.3 %collective-permute-start.32 = (f32[512,256]{1,0:T(8,128)S(1)}, f32[512,256]{1,0:T(8,128)}, u32[]{:S(2)}, u32[]{:S(2)}) collective-permute-start(f32[512,256]{1,0:T(8,128)S(1)} %collective-permute-done.28.refs_6_), channel_id=1, source_target_pairs={{8,16},{16,8},{9,17},{17,9},{10,18},{18,10},{11,19},{19,11},{12,20... | collective-permute-start | bytes 1572872 | tf_op jit(solution)/shard_map/ppermute | solution.py:401
  31.6 80.4 %collective-permute-start.33 = (f32[512,256]{1,0:T(8,128)S(1)}, f32[512,256]{1,0:T(8,128)}, u32[]{:S(2)}, u32[]{:S(2)}) collective-permute-start(f32[512,256]{1,0:T(8,128)S(1)} %collective-permute-done.28.refs_6_), channel_id=1, source_target_pairs={{16,0},{8,24},{17,1},{9,25},{18,2},{10,26},{19,3},{11,27},{20,4},{... | collective-permute-start | bytes 1572872 | tf_op jit(solution)/shard_map/ppermute | solution.py:403
  35.5 76.5 %collective-permute-start.31 = (f32[512,256]{1,0:T(8,128)}, f32[512,256]{1,0:T(8,128)}, u32[]{:S(2)}, u32[]{:S(2)}) collective-permute-start(f32[512,256]{1,0:T(8,128)} %collective-permute-done.29.refs_5_), channel_id=1, source_target_pairs={{8,0},{16,24},{9,1},{17,25},{10,2},{18,26},{11,3},{19,27},{12,4},{... | collective-permute-start | bytes 1572872 | tf_op jit(solution)/shard_map/ppermute | solution.py:402
  37.6 0.7 copy-start.2
  38.3 7.5 %copy-start.6 = (f32[512,256]{1,0:T(8,128)S(1)}, f32[512,256]{1,0:T(8,128)}, u32[]{:S(2)}) copy-start(f32[512,256]{1,0:T(8,128)} %refs_5_.1) | copy-start | bytes 1572868
  45.8 5.1 %copy-start.8 = (s32[8,4]{0,1:T(4,128)S(1)}, s32[8,4]{0,1:T(4,128)}, u32[]{:S(2)}) copy-start(s32[8,4]{0,1:T(4,128)} %param.31) | copy-start | bytes 388
  48.9 2.0 %copy-start = (bf16[4,2,512,512]{3,2,1,0:T(8,128)(2,1)}, bf16[4,2,512,512]{3,2,1,0:T(8,128)(2,1)S(1)}, u32[]{:S(2)}) copy-start(bf16[4,2,512,512]{3,2,1,0:T(8,128)(2,1)S(1)} %left_products.13.refs_4_) | copy-start | bytes 12582916
  50.9 63.2 %copy-start.3 = (s32[8,4]{1,0:T(8,128)S(1)}, s32[8,4]{1,0:T(8,128)}, u32[]{:S(2)}) copy-start(s32[8,4]{1,0:T(8,128)} %copy.30.row_partner.refs_2_) | copy-start | bytes 388
  50.9 61.1 %collective-permute-start.4 = (f32[3,256,256]{2,1,0:T(8,128)}, f32[3,256,256]{2,1,0:T(8,128)}, u32[]{:S(2)}, u32[]{:S(2)}) collective-permute-start(f32[3,256,256]{2,1,0:T(8,128)} %get-tuple-element.296), channel_id=1, source_target_pairs={{0,16},{8,24},{16,0},{24,8},{1,17},{9,25},{17,1},{25,9},{2,18},{10... | collective-permute-start | bytes 2359304 | tf_op jit(solution)/shard_map/cond/branch_3_fun/ppermute | solution.py:386
  50.9 60.4 %collective-permute-start.5 = (f32[256,256]{1,0:T(8,128)}, f32[256,256]{1,0:T(8,128)S(1)}, u32[]{:S(2)}, u32[]{:S(2)}) collective-permute-start(f32[256,256]{1,0:T(8,128)} %get-tuple-element.297), channel_id=1, source_target_pairs={{0,16},{8,24},{16,0},{24,8},{1,17},{9,25},{17,1},{25,9},{2,18},{10... | collective-permute-start | bytes 786440 | tf_op jit(solution)/shard_map/cond/branch_3_fun/ppermute | solution.py:386
  112.0 2.0 %copy-start.5 = (bf16[4,2,512,512]{3,2,1,0:T(8,128)(2,1)}, bf16[4,2,512,512]{3,2,1,0:T(8,128)(2,1)S(1)}, u32[]{:S(2)}) copy-start(bf16[4,2,512,512]{3,2,1,0:T(8,128)(2,1)S(1)} %get-tuple-element.456) | copy-start | bytes 12582916
  114.0 2.2 %copy-start.1 = (bf16[4,2,512,512]{3,2,1,0:T(8,128)(2,1)S(1)}, bf16[4,2,512,512]{3,2,1,0:T(8,128)(2,1)}, u32[]{:S(2)}) copy-start(bf16[4,2,512,512]{3,2,1,0:T(8,128)(2,1)} %copy-done) | copy-start | bytes 12582916
  120.7 30.5 %copy-start.4 = (s32[16]{0:T(128)S(1)}, s32[16]{0:T(128)}, u32[]{:S(2)}) copy-start(s32[16]{0:T(128)} %get-tuple-element.437.refs_1_) | copy-start | bytes 196
  120.7 30.5 %collective-permute-start.12 = (f32[3,256,256]{2,1,0:T(8,128)}, f32[3,256,256]{2,1,0:T(8,128)}, u32[]{:S(2)}, u32[]{:S(2)}) collective-permute-start(f32[3,256,256]{2,1,0:T(8,128)} %get-tuple-element.350), channel_id=1, source_target_pairs={{0,16},{8,24},{16,0},{24,8},{1,17},{9,25},{17,1},{25,9},{2,18},{10... | collective-permute-start | bytes 2359304 | tf_op jit(solution)/shard_map/cond/branch_2_fun/ppermute | solution.py:386
  151.3 27.6 %copy-start.7 = (f32[512,512]{1,0:T(8,128)S(1)}, f32[512,512]{1,0:T(8,128)}, u32[]{:S(2)}) copy-start(f32[512,512]{1,0:T(8,128)} %get-tuple-element.458.refs_4_) | copy-start | bytes 3145732
  154.0 24.8 %collective-permute-start.21 = (f32[512,512]{1,0:T(8,128)S(1)}, f32[512,512]{1,0:T(8,128)}, u32[]{:S(2)}, u32[]{:S(2)}) collective-permute-start(f32[512,512]{1,0:T(8,128)S(1)} %param.15), channel_id=1, source_target_pairs={{0,4},{1,5},{2,6},{3,7},{4,0},{5,1},{6,2},{7,3},{8,12},{9,13},{10,... | collective-permute-start | bytes 3145736 | tf_op jit(solution)/shard_map/cond/branch_3_fun/ppermute | solution.py:386
where the time goes:
time: 182 us; the launch traced here: 184 us
  waiting for transfers between devices  96.2 us (53%)
  Pallas kernels  39.3 us (22%)
  starting transfers between devices  19.3 us (11%)
  local copies, waits for them, and re-layouts  13.7 us (8%)
  blocking collectives  9.85 us (5%)
  between operations  3.42 us (2%)
    ppermute x9, waiting for transfers between devices, flip(): return lax.ppermute(value, axis, [(i, i ^ mask) for i in range(size)])  96.2 us
    pallas_call x2, Pallas kernels, left_products(): pl.pallas_call(functools.partial(left_kernel, blocks, block_cols, per_ste...  15.3 us
    pallas_call x3, Pallas kernels, right_products(): pl.pallas_call(functools.partial(right_kernel, columns, block_cols, half_...  14.7 us
    all_gather x1, blocking collectives, body(): lax.all_gather(jnp.where(slot_ids[:, None] < counts[0], coords, -1), 'row...  9.85 us
    ppermute x9, starting transfers between devices, flip(): return lax.ppermute(value, axis, [(i, i ^ mask) for i in range(size)])  9.53 us
    unnamed x22, local copies, waits for them, and re-layouts  8.93 us
    pallas_call x2, Pallas kernels, sum_blocks(): pl.pallas_call(functools.partial(sum_kernel, columns, second, half_rows,...  7.46 us
    ppermute x1, starting transfers between devices, gather_prolong(): mate_handed = lax.ppermute(mate, axis, [(2, 0), (1, 3)])  3.87 us
  transfers between devices with their start and end apart: 13, of which 4 were waited for; matrix products, arithmetic and copies ran while one was open for 4% of the time, Pallas kernels for 15%

commit v1 on v0

--- a/solution.py
+++ b/solution.py
@@ -9,7 +9,8 @@
 
 F32 = jnp.float32
 BF16 = jnp.bfloat16
-VMEM_BYTES = 48 * 1024 * 1024
+VMEM_BYTES = 60 * 1024 * 1024
+SHORT = pl.CostEstimate(flops=0, bytes_accessed=0, transcendentals=0)
 PARAMS = pltpu.CompilerParams(vmem_limit_bytes=VMEM_BYTES)
 
 
@@ -43,23 +44,35 @@
     return ((mate > me[0]) if given else (me[0] > mate)).astype(jnp.int32)
 
 
-def tables_kernel(n_row, half_rows, block_cols, me, live, row_partner, slots, mate_slots, sizes):
+def tables_kernel(n_row, half_rows, block_cols, packed, choices, *refs):
+    me, row_partner, col_partner, live = refs[:4]
+    others = refs[4:-5]
+    slots, mate_slots, first, second, across = refs[-5:]
     columns = Columns(Columns.OWN, n_row, block_cols)
     mate = row_partner[me[1], me[0]]
-    places = slots.shape[0]
-    per_device = live.shape[0] // n_row
-    for table, row in ((slots, me[0]), (mate_slots, mate)):
-        for place in range(places):
-            table[place] = jnp.int32(-1)
+    distance = me[0] ^ mate
+    per_device = live.shape[0]
+
+    def fill(table, source, start):
         for slot in range(per_device):
-            block_row = live[row * per_device + slot, 0]
+            block_row = source[start + slot, 0]
 
             @pl.when(block_row >= 0)
             def _():
-                table[block_row * block_cols + live[row * per_device + slot, 1]] = jnp.int32(slot)
+                table[block_row * block_cols + source[start + slot, 1]] = jnp.int32(slot)
+
+    for place in range(slots.shape[0]):
+        slots[place] = jnp.int32(-1)
+        mate_slots[place] = jnp.int32(-1)
+    fill(slots, live, 0)
+    if len(others) == 1:
+        fill(mate_slots, others[0], mate * per_device)
+    else:
+        for index, other in enumerate(others):
+            pl.when(distance == index + 1)(functools.partial(fill, mate_slots, other, 0))
 
     half_cols = columns.half_cols
-    for chunk in range(2):
+    for chunk, branch in enumerate((first, second)):
         counts = []
         for table, row, given in ((slots, me[0], True), (mate_slots, mate, False)):
             first_row = half_of(given, me, row_partner) * half_rows
@@ -69,19 +82,22 @@
                 place = (first_row + index % half_rows) * block_cols + first_col + index // half_rows
                 count = count + (table[place] >= 0).astype(jnp.int32)
             counts.append(count)
-        sizes[chunk] = jnp.maximum(*counts)
-
-
-def make_tables(me, live, row_partner, n_row, half_rows, block_cols):
+        choice = jnp.clip(jnp.maximum(*counts) - packed, 0, choices - 1)
+        branch[0] = (distance - 1) * choices + choice
+    across[0] = (me[1] ^ col_partner[me[0], me[1]]) - 1
+
+
+def make_tables(me, row_partner, col_partner, live, others, n_row, half_rows, block_cols, packed, choices):
     smem = pl.BlockSpec(memory_space=pltpu.SMEM)
     places = 2 * half_rows * block_cols
     return pl.pallas_call(
-        functools.partial(tables_kernel, n_row, half_rows, block_cols),
-        in_specs=[smem] * 3,
-        out_specs=[smem] * 3,
-        out_shape=[jax.ShapeDtypeStruct((n,), jnp.int32) for n in (places, places, 2)],
+        functools.partial(tables_kernel, n_row, half_rows, block_cols, packed, choices),
+        in_specs=[smem] * (4 + len(others)),
+        out_specs=[smem] * 5,
+        out_shape=[jax.ShapeDtypeStruct((n,), jnp.int32) for n in (places, places, 1, 1, 1)],
+        cost_estimate=SHORT,
         name="make_tables",
-    )(me, live, row_partner)
+    )(me, row_partner, col_partner, live, *others)
 
 
 class ChipBlocks:
@@ -181,11 +197,7 @@
         ),
         out_shape=jax.ShapeDtypeStruct((block_cols, 2, half_rows * width, tile_order), BF16),
         compiler_params=PARAMS,
-        cost_estimate=pl.CostEstimate(
-            flops=12 * half_rows * block_cols * width * tile_order * tile_order,
-            bytes_accessed=4 * half_rows * block_cols * tile_order * (tile_order + width),
-            transcendentals=0,
-        ),
+        cost_estimate=SHORT,
         name="left_products",
     )(me, slots, row_partner, *[tiles] * per_step, *blocks.operands)
 
@@ -210,6 +222,10 @@
 
     def column(self, step, me, col_partner):
         return self.half(step, me, col_partner) * self.half_cols + rem(step, self.half_cols)
+
+
+def packed_first(blocks):
+    return max(1, blocks * 3 // 4)
 
 
 def packed_place(slots, first_row, first_col, half_rows, half_cols, block_cols, block):
@@ -223,26 +239,21 @@
     return jnp.where(here == 1, before, count + block - before), here == 1
 
 
-def right_kernel(columns, block_cols, half_rows, shard_places, groups, *refs):
+def right_kernel(columns, block_cols, half_rows, places, *refs):
     me, slots, row_partner, col_partner, w_ref = refs[:5]
-    pieces = refs[5 : 5 + sum(groups)]
+    pieces = refs[5 : 5 + len(places)]
     step = pl.program_id(0)
     tile_order = w_ref.shape[3]
-    depth, width = pieces[0].shape
+    depth, width = pieces[0].shape[-2:]
     packs = columns.kind != Columns.KEPT
-    outs = refs[5 + sum(groups) : -3 if packs else -2]
+    outs = refs[5 + len(places) : -3 if packs else -2]
     p_high, p_low = refs[-2:]
 
     @pl.when(step == 0)
     def _():
-        at = 0
-        for place, count in zip(shard_places(me), groups):
-            value = pieces[at][...]
-            for other in range(1, count):
-                value = value + pieces[at + other][...]
-            at += count
-            rows = pl.ds(pl.multiple_of(place * depth, depth), depth)
-            p_high[rows, :], p_low[rows, :] = split(value)
+        for place, piece in zip(places, pieces):
+            rows = pl.ds(pl.multiple_of(place(me) * depth, depth), depth)
+            p_high[rows, :], p_low[rows, :] = split(piece[...].reshape(depth, width))
 
     column = columns.column(step, me, col_partner)
     rows = pl.ds(pl.multiple_of(column * tile_order, tile_order), tile_order)
@@ -278,12 +289,11 @@
             out[...] = packed[count + index]
 
 
-def right_products(kind, me, slots, row_partner, col_partner, w, shards, shard_places, n_row, half_rows):
+def right_products(kind, me, slots, row_partner, col_partner, w, shards, n_row, half_rows):
     block_cols, _, height, tile_order = w.shape
     columns = Columns(kind, n_row, block_cols)
     half_cols = columns.half_cols
-    depth, width = shards[0][0].shape
-    groups = [len(shard) for shard in shards]
+    depth, width = shards[0][0].shape[-2:]
     blocks = half_rows * half_cols
     p_rows = block_cols * tile_order
 
@@ -294,35 +304,38 @@
         return pl.BlockSpec(
             (height, width), lambda i, *_: (0, jnp.clip(i - first, 0, half_cols - 1))
         )
+
+    def shard_spec(array, place):
+        if array.ndim == 2:
+            return pl.BlockSpec((depth, width), lambda i, *_: (0, 0))
+        return pl.BlockSpec((1, depth, width), lambda i, me, *_: (place(me), 0, 0))
 
     scratch = [pltpu.VMEM((p_rows, width), BF16)] * 2
     if kind == Columns.KEPT:
         shapes = [(height, half_cols * width)] * 2
         out_specs = [quarter(0), quarter(half_cols)]
     else:
-        most = max(1, blocks * 3 // 4)
+        most = packed_first(blocks)
         shapes = [(most, width, width)] + [(width, width)] * (blocks - most)
         out_specs = [pl.BlockSpec(shape, lambda i, *_, n=len(shape): (0,) * n) for shape in shapes]
         scratch = [pltpu.VMEM((blocks, width, width), F32)] + scratch
     return pl.pallas_call(
-        functools.partial(right_kernel, columns, block_cols, half_rows, shard_places, groups),
+        functools.partial(
+            right_kernel, columns, block_cols, half_rows, [place for _, place in shards]
+        ),
         grid_spec=pltpu.PrefetchScalarGridSpec(
             num_scalar_prefetch=4,
             grid=(columns.steps,),
             in_specs=[pl.BlockSpec((1, 2, height, tile_order), w_at)]
-            + [pl.BlockSpec(memory_space=pltpu.VMEM)] * sum(groups),
+            + [shard_spec(array, place) for array, place in shards],
             out_specs=out_specs,
             scratch_shapes=scratch,
         ),
         out_shape=[jax.ShapeDtypeStruct(shape, F32) for shape in shapes],
         compiler_params=PARAMS,
-        cost_estimate=pl.CostEstimate(
-            flops=6 * columns.steps * height * width * tile_order,
-            bytes_accessed=4 * columns.steps * height * (tile_order + width),
-            transcendentals=0,
-        ),
+        cost_estimate=SHORT,
         name="right_products",
-    )(me, slots, row_partner, col_partner, w, *[piece for shard in shards for piece in shard])
+    )(me, slots, row_partner, col_partner, w, *[array for array, _ in shards])
 
 
 def sum_kernel(columns, second, half_rows, block_cols, arrays, *refs):
@@ -386,27 +399,20 @@
     return lax.ppermute(value, axis, [(i, i ^ mask) for i in range(size)])
 
 
-def near_prolong(shard, axis, size):
-    if size != 4:
-        return []
-    return [flip(shard, axis, size, 1), lax.ppermute(shard, axis, [(1, 2), (2, 1)])]
-
-
-def gather_prolong(shard, near, axis, size):
-    if size != 4:
-        gathered = lax.all_gather(shard, axis)
-        every = [[gathered[i]] for i in range(size)], lambda me: list(range(size))
-        return every, every
-    mate, over = near
-    mate_over = lax.ppermute(mate, axis, [(1, 2), (2, 1)])
-    handed = lax.ppermute(over, axis, [(1, 0), (2, 3)])
-    mate_handed = lax.ppermute(mate, axis, [(2, 0), (1, 3)])
-
-    def far_places(me):
-        return [jnp.where(me[0] < 2, 2, 1), jnp.where(me[0] < 2, 3, 0)]
-
-    own = [[shard], [mate]], lambda me: [me[0], me[0] ^ 1]
-    return own, ([[over, handed], [mate_over, mate_handed]], far_places)
+def gather_prolong(shard, mate, axis, size):
+    gathered = lax.all_gather(shard, axis)
+
+    def at(place):
+        return gathered, place
+
+    def side(other, index):
+        return at(lambda me: (div(2 * me[0], size) ^ other) * (size // 2) + index)
+
+    own = [side(0, index) for index in range(size // 2)]
+    if mate is not None:
+        own = [(shard, lambda me: me[0]), (mate, lambda me: me[0] ^ 1)]
+    far = [side(1, index) for index in range(size // 2)]
+    return own, far, [at(lambda me, index=index: jnp.int32(index)) for index in range(size)]
 
 
 def chip_restrict(shard, axis, size):
@@ -415,11 +421,11 @@
     return [shard, over_x, over_y, flip(over_x, axis, size, 4)]
 
 
-def pair_switch(mine, mate, size, branch, operand, sizes=(None,), choice=0):
-    branches = [functools.partial(branch, mask, each) for mask in range(1, size) for each in sizes]
-    if len(branches) == 1:
-        return branches[0](operand)
-    return lax.switch(((mine ^ mate) - 1) * len(sizes) + choice, branches, operand)
+def pair_switch(index, size, branch, operand, choices=1):
+    branches = [
+        functools.partial(branch, mask, choice) for mask in range(1, size) for choice in range(choices)
+    ]
+    return lax.switch(index[0], branches, operand)
 
 
 def solution(mesh):
@@ -435,24 +441,29 @@
         col = lax.axis_index("col").astype(jnp.int32)
         me = jnp.stack([row, col])
 
-        row_mate = row_partner[col, row]
-        col_mate = col_partner[row, col]
-
         slot_ids = jnp.arange(tiles.shape[0], dtype=jnp.int32)
-        live = lax.all_gather(
-            jnp.where(slot_ids[:, None] < counts[0], coords, -1), "row", axis=0, tiled=True
+        live = jnp.where(slot_ids[:, None] < counts[0], coords, -1)
+        if n_row == 4:
+            others = [flip(live, "row", n_row, mask) for mask in range(1, n_row)]
+        else:
+            others = [lax.all_gather(live, "row", axis=0, tiled=True)]
+        mate_prolong = flip(prolong, "row", n_row, 1) if n_row == 4 else None
+        prolong, others = lax.optimization_barrier((prolong, others))
+        packed = packed_first(half_rows * half_cols)
+        choices = half_rows * half_cols - packed + 1
+        slots, mate_slots, first, second, across = make_tables(
+            me, row_partner, col_partner, live, others, n_row, half_rows, block_cols, packed, choices
         )
-        near = near_prolong(prolong, "row", n_row)
-        slots, mate_slots, sizes = make_tables(me, live, row_partner, n_row, half_rows, block_cols)
         by_chip = n_col == 8 and block_rows == 4 and tile_order == 2 * restrict.shape[0]
         if by_chip:
             pieces = chip_restrict(restrict, "col", n_col)
-            pieces, near, slots = lax.optimization_barrier((pieces, near, slots))
+            pieces, slots, mate_prolong = lax.optimization_barrier((pieces, slots, mate_prolong))
             mine = jnp.stack(pieces)
             q_pieces = [mine, flip(mine, "col", n_col, 1)]
         else:
             q_rows = lax.all_gather(restrict, "col", axis=0, tiled=True)
-        own_shards, far_shards = gather_prolong(prolong, near, "row", n_row)
+
+        own_shards, far_shards, all_shards = gather_prolong(prolong, mate_prolong, "row", n_row)
 
         def left(given):
             if by_chip:
@@ -461,9 +472,9 @@
                 blocks = WholeBlocks(given, q_rows, tile_order, half_rows)
             return left_products(me, slots, row_partner, tiles, blocks, half_rows, block_cols)
 
-        def right(kind, w, shards, places):
+        def right(kind, w, shards):
             return right_products(
-                kind, me, slots, row_partner, col_partner, w, shards, places, n_row, half_rows
+                kind, me, slots, row_partner, col_partner, w, shards, n_row, half_rows
             )
 
         def swap_chunk(beside, mask, extra, chunk):
@@ -476,26 +487,20 @@
         def swap_section(mask, _, section):
             return flip(section, "col", n_col, mask)
 
-        def exchange(size, chunk, beside):
-            choice = jnp.clip(size - chunk[0].shape[0], 0, len(chunk) - 1)
+        def exchange(index, chunk, beside):
             branch = functools.partial(swap_chunk, beside)
-            return pair_switch(row, row_mate, n_row, branch, chunk, tuple(range(len(chunk))), choice)
+            return pair_switch(index, n_row, branch, chunk, choices)
 
         w = left(True)
-        own = right(Columns.OWN, w, *own_shards)
-        own, w_kept = exchange(sizes[0], own, lambda: left(False))
-        far_pieces, own = lax.optimization_barrier((far_shards[0], own))
-        far = right(Columns.FAR, w, far_pieces, far_shards[1])
-        if n_row == 4:
-            every = own_shards[0] + far_pieces, lambda me: own_shards[1](me) + far_shards[1](me)
-        else:
-            every = own_shards
-        far, kept = exchange(sizes[1], far, lambda: right(Columns.KEPT, w_kept, *every))
+        own = right(Columns.OWN, w, own_shards)
+        own, w_kept = exchange(first, own, lambda: left(False))
+        far = right(Columns.FAR, w, far_shards)
+        far, kept = exchange(second, far, lambda: right(Columns.KEPT, w_kept, all_shards))
         chunks = list(own) + list(far)
         add = functools.partial(sum_blocks, n_row=n_row, half_rows=half_rows, block_cols=block_cols)
         tables = (me, mate_slots, row_partner, col_partner)
         section = add(False, tables, kept=kept[0], chunks=chunks)
-        section = pair_switch(col, col_mate, n_col, swap_section, section)
+        section = pair_switch(across, n_col, swap_section, section)
         return add(True, tables, kept=kept[1], chunks=chunks, section=section)
 
     in_specs = (

time: 182 us -> 197 us (1.082)
  the two profiles are of different devices: /device:TPU:22 before, /device:TPU:31 now
where the time goes in v1:
time: 197 us; the launch traced here: 198 us
  starting transfers between devices  73.8 us (37%)
  waiting for transfers between devices  58.3 us (30%)
  Pallas kernels  43.9 us (22%)
  between operations  15.9 us (8%)
  local copies, waits for them, and re-layouts  5.11 us (3%)
    ppermute x12, starting transfers between devices, flip(): return lax.ppermute(value, axis, [(i, i ^ mask) for i in range(size)])  73.8 us
    ppermute x12, waiting for transfers between devices, flip(): return lax.ppermute(value, axis, [(i, i ^ mask) for i in range(size)])  58.3 us
    pallas_call x2, Pallas kernels, left_products(): pl.pallas_call(functools.partial(left_kernel, blocks, block_cols, per_ste...  17.9 us
    pallas_call x3, Pallas kernels, right_products(): pl.pallas_call(functools.partial(right_kernel, columns, block_cols, half_...  16.1 us
    pallas_call x2, Pallas kernels, sum_blocks(): pl.pallas_call(functools.partial(sum_kernel, columns, second, half_rows,...  7.84 us
  transfers between devices with their start and end apart: 13, of which 8 were waited for; matrix products, arithmetic and copies ran while one was open for 2% of the time, Pallas kernels for 16%

profile of v1, /device:TPU:31, one launch (start us, length us, event | category | flops | bytes accessed | tf_op | source)
XLA Modules:
  0.0 198.4 jit_solution(4879571694360772114)
XLA Ops:
  7.2 0.8 copy.8
  8.1 1.3 collective-permute-start.26
  9.4 2.2 %collective-permute-start.25 = (s32[16,2]{1,0:T(8,128)S(1)}, s32[16,2]{1,0:T(8,128)S(1)}, u32[]{:S(2)}, u32[]{:S(2)}) collective-permute-start(s32[16,2]{1,0:T(8,128)S(1)} %broadcast_select_fusion.refs_3_), channel_id=1, source_target_pairs={{0,8},{8,0},{16,24},{24,16},{1,9},{9,1},{17,25},{25,17},{2,10},{10... | collective-permute-start | bytes 392 | tf_op jit(solution)/shard_map/ppermute | solution.py:399
  11.6 0.8 collective-permute-done.27.refs_6_
  12.4 0.6 collective-permute-done.25.refs_4_
  13.3 1.2 collective-permute-start.31
  14.7 4.5 %collective-permute-done.28 = f32[256,256]{1,0:T(8,128)S(1)} collective-permute-done((f32[256,256]{1,0:T(8,128)}, f32[256,256]{1,0:T(8,128)S(1)}, u32[]{:S(2)}, u32[]{:S(2)}) %collective-permute-start.28) | collective-permute-done | bytes 262176 | tf_op jit(solution)/shard_map/ppermute | solution.py:399
  19.4 1.3 copy.9.refs_1_.refs_2_
  20.9 2.0 %make_tables.1 = (s32[16]{0:T(128)S(1)}, s32[16]{0:T(128)}, s32[1]{0:T(128)}, s32[1]{0:T(128)}, s32[1]{0:T(128)}) custom-call(s32[2]{0:T(128)S(1)} %pad_add_fusion.refs_0_, s32[8,4]{1,0:T(8,128)} %copy.9.refs_1_.refs_2_, s32[4,8]{1,0:T(4,128)} %refs_3_.9, s32[16,2]{1,0:T(8,128)} %copy-done.6, s32[16,2]{1,0:T(8,128)} %copy-done.9, s32[16,2]{1,0:T(8,128)} %copy-done.8, ...), custom_call_target="tpu_custom_call" | custom-call | tf_op jit(solution)/shard_map/make_tables/pallas_call | solution.py:93
  22.9 4.7 %collective-permute-done.30 = f32[256,256]{1,0:T(8,128)S(1)} collective-permute-done((f32[256,256]{1,0:T(8,128)S(1)}, f32[256,256]{1,0:T(8,128)S(1)}, u32[]{:S(2)}, u32[]{:S(2)}) %collective-permute-start.30) | collective-permute-done | bytes 262176 | tf_op jit(solution)/shard_map/ppermute | solution.py:399
  27.7 1.2 pad_maximum_fusion.refs_5_
  28.9 10.5 %collective-permute-start.32 = (f32[4,256,256]{2,1,0:T(8,128)S(1)}, f32[4,256,256]{2,1,0:T(8,128)S(1)}, u32[]{:S(2)}, u32[]{:S(2)}) collective-permute-start(f32[4,256,256]{2,1,0:T(8,128)S(1)} %pad_maximum_fusion.refs_5_), channel_id=1, source_target_pairs={{0,1},{1,0},{2,3},{3,2},{4,5},{5,4},{6,7},{7,6},{8,9},{9,8},{10,11... | collective-permute-start | bytes 3145736 | tf_op jit(solution)/shard_map/ppermute | solution.py:399
  41.7 8.9 %left_products.13.refs_4_ = bf16[4,2,512,512]{3,2,1,0:T(8,128)(2,1)} custom-call(s32[2]{0:T(128)S(1)} %pad_add_fusion.refs_0_, s32[16]{0:T(128)S(1)} %get-tuple-element.352.refs_1_, s32[8,4]{1,0:T(8,128)} %copy.9.refs_1_.refs_2_, f32[16,512,512]{2,1,0:T(8,128)} %refs_4_.1, f32[16,512,512]{2,1,0:T(8,128)} %refs_4_.1, ...), custom_call_target="tpu_custom_call" | custom-call | tf_op jit(solution)/shard_map/left_products/pallas_call | solution.py:189
  50.6 4.8 %right_products.15 = (f32[3,256,256]{2,1,0:T(8,128)}, f32[256,256]{1,0:T(8,128)S(1)}) custom-call(s32[2]{0:T(128)S(1)} %pad_add_fusion.refs_0_, s32[16]{0:T(128)S(1)} %get-tuple-element.352.refs_1_, s32[8,4]{1,0:T(8,128)} %copy.9.refs_1_.refs_2_, s32[4,8]{1,0:T(4,128)S(1)} %copy-done.5, bf16[4,2,512,512]{3,2,1,0:T(8,128)(2,1)} %left_products.13.refs_4_, ...), custom_call_target="tpu_custom_call" | custom-call | tf_op jit(solution)/shard_map/right_products/pallas_call | solution.py:322
  55.3 23.6 %conditional.3 = (f32[3,256,256]{2,1,0:T(8,128)}, f32[256,256]{1,0:T(8,128)S(1)}, bf16[4,2,512,512]{3,2,1,0:T(8,128)(2,1)}) conditional(s32[]{:T(128)} %bitcast.9, (f32[3,256,256]{2,1,0:T(8,128)}, s32[2]{0:T(128)S(1)}, s32[16]{0:T(128)S(1)}, s32[8,4]{0,1:T(4,128)S(1)}, f32[16,512,512]{2,1,0:T(8,128)}, ...), branch_computations={%region_0.1_spmd, %region_1.2_spmd, %region_2.3_spmd, %region_3.4_... | conditional | bytes 4718952 | solution.py:428
  55.3 4.9 %collective-permute-start.6 = (f32[3,256,256]{2,1,0:T(8,128)}, f32[3,256,256]{2,1,0:T(8,128)}, u32[]{:S(2)}, u32[]{:S(2)}) collective-permute-start(f32[3,256,256]{2,1,0:T(8,128)} %get-tuple-element.244), channel_id=1, source_target_pairs={{0,24},{8,16},{16,8},{24,0},{1,25},{9,17},{17,9},{25,1},{2,26},{10... | collective-permute-start | bytes 2359304 | tf_op jit(solution)/shard_map/cond/branch_4_fun/ppermute | solution.py:399
  60.2 0.7 copy.17.refs_2_
  60.9 8.9 %left_products.11 = bf16[4,2,512,512]{3,2,1,0:T(8,128)(2,1)} custom-call(s32[2]{0:T(128)S(1)} %get-tuple-element.246.refs_0_, s32[16]{0:T(128)S(1)} %get-tuple-element.247.refs_1_, s32[8,4]{1,0:T(8,128)} %copy.17.refs_2_, f32[16,512,512]{2,1,0:T(8,128)} %get-tuple-element.249.refs_3_.refs_4_, f32[16,512,512]{2,1,0:T(8,128)} %get-tuple-element.249.refs_3_.refs_4_, ...), custom_call_target="tpu_custom_call" | custom-call | tf_op jit(solution)/shard_map/cond/branch_4_fun/left_products/pallas_call | solution.py:189
  69.8 9.1 %collective-permute-done.6 = f32[3,256,256]{2,1,0:T(8,128)} collective-permute-done((f32[3,256,256]{2,1,0:T(8,128)}, f32[3,256,256]{2,1,0:T(8,128)}, u32[]{:S(2)}, u32[]{:S(2)}) %collective-permute-start.6) | collective-permute-done | bytes 786464 | tf_op jit(solution)/shard_map/cond/branch_4_fun/ppermute | solution.py:399
  79.0 0.7 copy-done.1
  79.7 4.8 %right_products.14 = (f32[3,256,256]{2,1,0:T(8,128)}, f32[256,256]{1,0:T(8,128)S(1)}) custom-call(s32[2]{0:T(128)S(1)} %pad_add_fusion.refs_0_, s32[16]{0:T(128)S(1)} %get-tuple-element.352.refs_1_, s32[8,4]{1,0:T(8,128)} %copy.9.refs_1_.refs_2_, s32[4,8]{1,0:T(4,128)S(1)} %copy-done.5, bf16[4,2,512,512]{3,2,1,0:T(8,128)(2,1)} %left_products.13.refs_4_, ...), custom_call_target="tpu_custom_call" | custom-call | tf_op jit(solution)/shard_map/right_products/pallas_call | solution.py:322
  84.5 26.9 %conditional.4 = (f32[3,256,256]{2,1,0:T(8,128)}, f32[256,256]{1,0:T(8,128)S(1)}, f32[512,512]{1,0:T(8,128)S(1)}, f32[512,512]{1,0:T(8,128)}) conditional(s32[]{:T(128)} %bitcast.3, (f32[3,256,256]{2,1,0:T(8,128)}, s32[2]{0:T(128)S(1)}, s32[16]{0:T(128)S(1)}, s32[8,4]{0,1:T(4,128)S(1)}, s32[4,8]{1,0:T(4,128)S(1)}, ...), branch_computations={%region_6.7_spmd, %region_7.8_spmd, %region_8.9_spmd, %region_9.10... | conditional | bytes 4718960 | solution.py:428
  84.5 3.7 %collective-permute-start.16 = (f32[3,256,256]{2,1,0:T(8,128)}, f32[3,256,256]{2,1,0:T(8,128)}, u32[]{:S(2)}, u32[]{:S(2)}) collective-permute-start(f32[3,256,256]{2,1,0:T(8,128)} %get-tuple-element.310), channel_id=1, source_target_pairs={{0,24},{8,16},{16,8},{24,0},{1,25},{9,17},{17,9},{25,1},{2,26},{10... | collective-permute-start | bytes 2359304 | tf_op jit(solution)/shard_map/cond/branch_5_fun/ppermute | solution.py:399
  88.2 0.7 copy.24.refs_2_
  88.9 6.6 %right_products.13 = (f32[512,512]{1,0:T(8,128)S(1)}, f32[512,512]{1,0:T(8,128)}) custom-call(s32[2]{0:T(128)S(1)} %get-tuple-element.312.refs_0_, s32[16]{0:T(128)S(1)} %get-tuple-element.313.refs_1_, s32[8,4]{1,0:T(8,128)} %copy.24.refs_2_, s32[4,8]{1,0:T(4,128)S(1)} %get-tuple-element.315.refs_3_, bf16[4,2,512,512]{3,2,1,0:T(8,128)(2,1)} %get-tuple-element.316.refs_4_, ...), custom_call_target="tpu_custom_call" | custom-call | tf_op jit(solution)/shard_map/cond/branch_5_fun/right_products/pallas_call | solution.py:322
  95.4 15.0 %collective-permute-done.17 = f32[256,256]{1,0:T(8,128)} collective-permute-done((f32[256,256]{1,0:T(8,128)S(1)}, f32[256,256]{1,0:T(8,128)}, u32[]{:S(2)}, u32[]{:S(2)}) %collective-permute-start.17) | collective-permute-done | bytes 262176 | tf_op jit(solution)/shard_map/cond/branch_5_fun/ppermute | solution.py:399
  110.4 0.9 copy.66
  111.4 2.9 %sum_blocks.2 = f32[512,512]{1,0:T(8,128)S(1)} custom-call(s32[2]{0:T(128)S(1)} %pad_add_fusion.refs_0_, s32[16]{0:T(128)} %get-tuple-element.349.refs_1_, s32[8,4]{1,0:T(8,128)} %copy.9.refs_1_.refs_2_, s32[4,8]{1,0:T(4,128)S(1)} %copy-done.5, f32[512,512]{1,0:T(8,128)S(1)} %get-tuple-element.371.refs_4_, f32[3,256,256]{2,1,0:T(8,128)} %get-tuple-element.366.refs_5_, ...), custom_call_target="tpu_custom_call" | custom-call | tf_op jit(solution)/shard_map/sum_blocks/pallas_call | solution.py:382
  114.3 72.3 %conditional.5 = (f32[512,512]{1,0:T(8,128)}) conditional(s32[]{:T(128)} %bitcast.10, f32[512,512]{1,0:T(8,128)S(1)} %sum_blocks.2, f32[512,512]{1,0:T(8,128)S(1)} %sum_blocks.2, f32[512,512]{1,0:T(8,128)S(1)} %sum_blocks.2, f32[512,512]{1,0:T(8,128)S(1)} %sum_blocks.2, f32[512,512]{1,0:T(8,128)S(1)} %sum_blocks.2, ...), branch_computations={%region_12.13_spmd, %region_13.14_spmd, %region_14.15_spmd, %regio... | conditional | bytes 4194352 | solution.py:428
  114.3 49.2 %collective-permute-start.24 = (f32[512,512]{1,0:T(8,128)S(1)}, f32[512,512]{1,0:T(8,128)}, u32[]{:S(2)}, u32[]{:S(2)}) collective-permute-start(f32[512,512]{1,0:T(8,128)S(1)} %param.18), channel_id=1, source_target_pairs={{0,7},{1,6},{2,5},{3,4},{4,3},{5,2},{6,1},{7,0},{8,15},{9,14},{10,... | collective-permute-start | bytes 3145736 | tf_op jit(solution)/shard_map/cond/branch_6_fun/ppermute | solution.py:399
  163.5 23.2 %collective-permute-done.24 = f32[512,512]{1,0:T(8,128)} collective-permute-done((f32[512,512]{1,0:T(8,128)S(1)}, f32[512,512]{1,0:T(8,128)}, u32[]{:S(2)}, u32[]{:S(2)}) %collective-permute-start.24) | collective-permute-done | bytes 1048608 | tf_op jit(solution)/shard_map/cond/branch_6_fun/ppermute | solution.py:399
  186.6 4.9 %sum_blocks.3 = f32[512,512]{1,0:T(8,128)} custom-call(s32[2]{0:T(128)S(1)} %pad_add_fusion.refs_0_, s32[16]{0:T(128)} %get-tuple-element.349.refs_1_, s32[8,4]{1,0:T(8,128)} %copy.9.refs_1_.refs_2_, s32[4,8]{1,0:T(4,128)S(1)} %copy-done.5, f32[512,512]{1,0:T(8,128)} %get-tuple-element.365.refs_4_, f32[3,256,256]{2,1,0:T(8,128)} %get-tuple-element.366.refs_5_, ...), custom_call_target="tpu_custom_call" | custom-call | tf_op jit(solution)/shard_map/sum_blocks/pallas_call | solution.py:382
  (35 shorter events, 1.5 us)
Async XLA Ops:
  6.5 72.4 %all-gather.3.cloned.1.call-start = ((), (), s32[]{:S(2)}) async-start(), calls=%async_computation | async-start | bytes 2621440 | tf_op jit(solution)/shard_map/all_gather | solution.py:403
  8.0 12.8 %copy-start.6 = (s32[16,2]{1,0:T(8,128)}, s32[16,2]{1,0:T(8,128)S(1)}, u32[]{:S(2)}) copy-start(s32[16,2]{1,0:T(8,128)S(1)} %broadcast_select_fusion.refs_3_) | copy-start | bytes 388
  8.0 4.3 %collective-permute-start.27 = (s32[16,2]{1,0:T(8,128)S(1)}, s32[16,2]{1,0:T(8,128)S(1)}, u32[]{:S(2)}, u32[]{:S(2)}) collective-permute-start(s32[16,2]{1,0:T(8,128)S(1)} %broadcast_select_fusion.refs_3_), channel_id=1, source_target_pairs={{0,24},{8,16},{16,8},{24,0},{1,25},{9,17},{17,9},{25,1},{2,26},{10... | collective-permute-start | bytes 392 | tf_op jit(solution)/shard_map/ppermute | solution.py:399
  8.1 4.3 %collective-permute-start.26 = (s32[16,2]{1,0:T(8,128)S(1)}, s32[16,2]{1,0:T(8,128)S(1)}, u32[]{:S(2)}, u32[]{:S(2)}) collective-permute-start(s32[16,2]{1,0:T(8,128)S(1)} %broadcast_select_fusion.refs_3_), channel_id=1, source_target_pairs={{0,16},{8,24},{16,0},{24,8},{1,17},{9,25},{17,1},{25,9},{2,18},{10... | collective-permute-start | bytes 392 | tf_op jit(solution)/shard_map/ppermute | solution.py:399
  9.4 3.5 %collective-permute-start.25 = (s32[16,2]{1,0:T(8,128)S(1)}, s32[16,2]{1,0:T(8,128)S(1)}, u32[]{:S(2)}, u32[]{:S(2)}) collective-permute-start(s32[16,2]{1,0:T(8,128)S(1)} %broadcast_select_fusion.refs_3_), channel_id=1, source_target_pairs={{0,8},{8,0},{16,24},{24,16},{1,9},{9,1},{17,25},{25,17},{2,10},{10... | collective-permute-start | bytes 392 | tf_op jit(solution)/shard_map/ppermute | solution.py:399
  12.3 8.5 %copy-start.7 = (s32[16,2]{1,0:T(8,128)}, s32[16,2]{1,0:T(8,128)S(1)}, u32[]{:S(2)}) copy-start(s32[16,2]{1,0:T(8,128)S(1)} %collective-permute-done.27.refs_6_) | copy-start | bytes 388
  12.4 8.5 %copy-start.8 = (s32[16,2]{1,0:T(8,128)}, s32[16,2]{1,0:T(8,128)S(1)}, u32[]{:S(2)}) copy-start(s32[16,2]{1,0:T(8,128)S(1)} %collective-permute-done.26.refs_5_) | copy-start | bytes 388
  12.9 8.0 %copy-start.9 = (s32[16,2]{1,0:T(8,128)}, s32[16,2]{1,0:T(8,128)S(1)}, u32[]{:S(2)}) copy-start(s32[16,2]{1,0:T(8,128)S(1)} %collective-permute-done.25.refs_4_) | copy-start | bytes 388
  13.0 6.3 %collective-permute-start.28 = (f32[256,256]{1,0:T(8,128)}, f32[256,256]{1,0:T(8,128)S(1)}, u32[]{:S(2)}, u32[]{:S(2)}) collective-permute-start(f32[256,256]{1,0:T(8,128)} %param.29), channel_id=1, source_target_pairs={{0,2},{1,3},{2,0},{3,1},{4,6},{5,7},{6,4},{7,5},{8,10},{9,11},{10,... | collective-permute-start | bytes 786440 | tf_op jit(solution)/shard_map/ppermute | solution.py:399
  13.3 14.4 %collective-permute-start.31 = (f32[512,256]{1,0:T(8,128)}, f32[512,256]{1,0:T(8,128)S(1)}, u32[]{:S(2)}, u32[]{:S(2)}) collective-permute-start(f32[512,256]{1,0:T(8,128)} %refs_5_), channel_id=1, source_target_pairs={{0,8},{8,0},{16,24},{24,16},{1,9},{9,1},{17,25},{25,17},{2,10},{10... | collective-permute-start | bytes 1572872 | tf_op jit(solution)/shard_map/ppermute | solution.py:399
  14.5 8.4 %collective-permute-start.29 = (f32[256,256]{1,0:T(8,128)}, f32[256,256]{1,0:T(8,128)S(1)}, u32[]{:S(2)}, u32[]{:S(2)}) collective-permute-start(f32[256,256]{1,0:T(8,128)} %param.29), channel_id=1, source_target_pairs={{0,4},{1,5},{2,6},{3,7},{4,0},{5,1},{6,2},{7,3},{8,12},{9,13},{10,... | collective-permute-start | bytes 786440 | tf_op jit(solution)/shard_map/ppermute | solution.py:399
  19.2 8.4 %collective-permute-start.30 = (f32[256,256]{1,0:T(8,128)S(1)}, f32[256,256]{1,0:T(8,128)S(1)}, u32[]{:S(2)}, u32[]{:S(2)}) collective-permute-start(f32[256,256]{1,0:T(8,128)S(1)} %collective-permute-done.28), channel_id=1, source_target_pairs={{0,4},{1,5},{2,6},{3,7},{4,0},{5,1},{6,2},{7,3},{8,12},{9,13},{10,... | collective-permute-start | bytes 786440 | tf_op jit(solution)/shard_map/ppermute | solution.py:399
  27.7 22.9 %copy-start.3 = (f32[512,256]{1,0:T(8,128)}, f32[512,256]{1,0:T(8,128)S(1)}, u32[]{:S(2)}) copy-start(f32[512,256]{1,0:T(8,128)S(1)} %collective-permute-done.31.refs_6_) | copy-start | bytes 1572868
  28.9 12.8 %collective-permute-start.32 = (f32[4,256,256]{2,1,0:T(8,128)S(1)}, f32[4,256,256]{2,1,0:T(8,128)S(1)}, u32[]{:S(2)}, u32[]{:S(2)}) collective-permute-start(f32[4,256,256]{2,1,0:T(8,128)S(1)} %pad_maximum_fusion.refs_5_), channel_id=1, source_target_pairs={{0,1},{1,0},{2,3},{3,2},{4,5},{5,4},{6,7},{7,6},{8,9},{9,8},{10,11... | collective-permute-start | bytes 3145736 | tf_op jit(solution)/shard_map/ppermute | solution.py:399
  41.2 9.4 %copy-start.5 = (s32[4,8]{1,0:T(4,128)S(1)}, s32[4,8]{1,0:T(4,128)}, u32[]{:S(2)}) copy-start(s32[4,8]{1,0:T(4,128)} %refs_3_.9) | copy-start | bytes 388
  50.6 4.8 %copy-start.4 = (s32[8,4]{0,1:T(4,128)S(1)}, s32[8,4]{0,1:T(4,128)}, u32[]{:S(2)}) copy-start(s32[8,4]{0,1:T(4,128)} %param.31) | copy-start | bytes 388
  55.3 23.6 %collective-permute-start.6 = (f32[3,256,256]{2,1,0:T(8,128)}, f32[3,256,256]{2,1,0:T(8,128)}, u32[]{:S(2)}, u32[]{:S(2)}) collective-permute-start(f32[3,256,256]{2,1,0:T(8,128)} %get-tuple-element.244), channel_id=1, source_target_pairs={{0,24},{8,16},{16,8},{24,0},{1,25},{9,17},{17,9},{25,1},{2,26},{10... | collective-permute-start | bytes 2359304 | tf_op jit(solution)/shard_map/cond/branch_4_fun/ppermute | solution.py:399
  79.0 0.7 copy-start.1
  79.7 4.8 %copy-start = (f32[2048,256]{1,0:T(8,128)S(1)}, f32[2048,256]{1,0:T(8,128)}, u32[]{:S(2)}) copy-start(f32[2048,256]{1,0:T(8,128)} %all-gather.3.cloned.1.call-done) | copy-start | bytes 6291460
  84.5 26.9 %collective-permute-start.16 = (f32[3,256,256]{2,1,0:T(8,128)}, f32[3,256,256]{2,1,0:T(8,128)}, u32[]{:S(2)}, u32[]{:S(2)}) collective-permute-start(f32[3,256,256]{2,1,0:T(8,128)} %get-tuple-element.310), channel_id=1, source_target_pairs={{0,24},{8,16},{16,8},{24,0},{1,25},{9,17},{17,9},{25,1},{2,26},{10... | collective-permute-start | bytes 2359304 | tf_op jit(solution)/shard_map/cond/branch_5_fun/ppermute | solution.py:399
  88.1 22.3 %collective-permute-start.17 = (f32[256,256]{1,0:T(8,128)S(1)}, f32[256,256]{1,0:T(8,128)}, u32[]{:S(2)}, u32[]{:S(2)}) collective-permute-start(f32[256,256]{1,0:T(8,128)S(1)} %get-tuple-element.311), channel_id=1, source_target_pairs={{0,24},{8,16},{16,8},{24,0},{1,25},{9,17},{17,9},{25,1},{2,26},{10... | collective-permute-start | bytes 786440 | tf_op jit(solution)/shard_map/cond/branch_5_fun/ppermute | solution.py:399
  111.4 75.3 %copy-start.2 = (f32[256,256]{1,0:T(8,128)S(1)}, f32[256,256]{1,0:T(8,128)}, u32[]{:S(2)}) copy-start(f32[256,256]{1,0:T(8,128)} %copy-done.1) | copy-start | bytes 786436
  114.3 72.3 %collective-permute-start.24 = (f32[512,512]{1,0:T(8,128)S(1)}, f32[512,512]{1,0:T(8,128)}, u32[]{:S(2)}, u32[]{:S(2)}) collective-permute-start(f32[512,512]{1,0:T(8,128)S(1)} %param.18), channel_id=1, source_target_pairs={{0,7},{1,6},{2,5},{3,4},{4,3},{5,2},{6,1},{7,0},{8,15},{9,14},{10,... | collective-permute-start | bytes 3145736 | tf_op jit(solution)/shard_map/cond/branch_6_fun/ppermute | solution.py:399
Sparse Core Ops, SparseCore 0:
  13.1 50.0 all-gather.2
